TPU v7x, 32 devices: a whole 2x2x4 slice. The times are simulated.
32 devices in a mesh: section: 2 (over z_hi), span: 8 (over y, x, core), seq: 2 (over z_lo).
Axes of the slice: x: 2, y: 2, z: 4 (z_hi: 2, z_lo: 2; z = z_hi * 2 + z_lo), core: 2. Of those that a mesh axis runs over, the one named last changes fastest.
Arguments:
- latents: bfloat16 [8064, 5120], P(('span', 'seq')), may hold values from -6 to 6
- queries: bfloat16 [2, 8064, 5120], P('section', ('span', 'seq')), may hold values from -12 to 12, as said below
- key_states: bfloat16 [2, 8064, 5120], P('section', ('span', 'seq')), may hold values from -12 to 12
- value_states: bfloat16 [2, 8064, 5120], P('section', ('span', 'seq')), may hold values from -6 to 6
- gate_scales: float32 [2, 5120], P('section'), may hold values from 4 to 12
- window: int32 [7], replicated, may hold values from 1 to 10, 38 in all
- intersection: int32 [7], replicated, may hold values from 1 to 10, 38 in all
- blend_index: int32 [7, 10], replicated, may hold values from 0 to 7
Outputs:
- denoised: bfloat16 [8064, 5120], P('span', ('section', 'seq'))
Inputs may be any that keep to these rules, and one draw needn't show every extreme that they name: `queries`: queries of the span lie in the stated range. `window`: 10 is reached in every draw. `intersection`: 10 is reached in every draw.
All inputs are finite; a program needn't handle non-finite values.
Results may differ from a plain program's by a relative error of at most 0.0095.
Values may be sent and summed in bfloat16 or wider, within the bound.
A program may use at most 192 MiB of HBM per device.

v0:
```python
import math

import jax
import jax.numpy as jnp
from jax import lax
from jax.sharding import PartitionSpec as P

HEADS = 40
HEAD_DIM = 128
TOK_FRAME = 48
BF = 10
WEIGHTS = 8


def from_behind(shard, axis, by):
    length = lax.axis_size(axis)
    pairs = [(i, i + by) for i in range(length) if 0 <= i + by < length]
    return lax.ppermute(shard, axis, pairs)


def attend(query_block, key_block, value_block, usable, head_count):
    row_count = query_block.shape[0]
    group_size = math.gcd(head_count, 4)
    group_width = group_size * HEAD_DIM
    score_scale = 1.0 / math.sqrt(HEAD_DIM)

    def head_block(block_id, result):
        offset = block_id * group_width
        query_part = lax.dynamic_slice_in_dim(query_block, offset, group_width, 1).reshape(
            row_count, group_size, HEAD_DIM
        )
        key_part = lax.dynamic_slice_in_dim(key_block, offset, group_width, 1).reshape(
            -1, group_size, HEAD_DIM
        )
        value_part = lax.dynamic_slice_in_dim(value_block, offset, group_width, 1).reshape(
            -1, group_size, HEAD_DIM
        )
        scores = (
            jnp.einsum("qhd,khd->hqk", query_part, key_part, preferred_element_type=jnp.float32)
            * score_scale
        )
        scores = jnp.where(usable[None, None, :], scores, -jnp.inf)
        row_max = jnp.max(scores, axis=-1, keepdims=True)
        lifted = jnp.exp(scores - row_max)
        row_sum = jnp.sum(lifted, axis=-1, keepdims=True)
        weights = (lifted / row_sum).astype(jnp.bfloat16)
        combined = jnp.einsum(
            "hqk,khd->qhd", weights, value_part, preferred_element_type=jnp.float32
        )
        combined = combined.astype(jnp.bfloat16).reshape(row_count, group_width)
        return lax.dynamic_update_slice_in_dim(result, combined, offset, 1)

    empty = jnp.zeros((row_count, head_count * HEAD_DIM), jnp.bfloat16)
    return lax.fori_loop(0, head_count // group_size, head_block, empty)


def finish_blend(second, intersection, blend_index, earlier, span_pos):
    tail_rows = BF * TOK_FRAME
    whole = lax.all_to_all(second, "seq", split_axis=1, concat_axis=0, tiled=True)
    previous = from_behind(whole[-tail_rows:], "span", 1)
    length = intersection[earlier]
    frame_ids = jnp.arange(BF)
    source = jnp.clip(BF - length + frame_ids, 0, BF - 1)
    picked = jnp.take(previous.reshape(BF, TOK_FRAME, -1), source, axis=0).astype(jnp.float32)
    weight = ((blend_index[earlier].astype(jnp.float32) + 0.5) / WEIGHTS)[:, None, None]
    active = (frame_ids < length) & (span_pos > 0)
    leading = whole[:tail_rows].reshape(BF, TOK_FRAME, -1).astype(jnp.float32)
    blended = jnp.where(active[:, None, None], weight * leading + (1.0 - weight) * picked, leading)
    blended = blended.astype(jnp.bfloat16).reshape(tail_rows, -1)
    return jnp.concatenate([blended, whole[tail_rows:]], 0)


def local(
    latents, queries, key_states, value_states, gate_scales, window, intersection, blend_index
):
    own_query = queries[0]
    own_key = key_states[0]
    own_value = value_states[0]
    gate_row = gate_scales[0]
    span_pos = lax.axis_index("span")
    section_pos = lax.axis_index("section")
    tail_rows = BF * TOK_FRAME
    earlier = jnp.maximum(span_pos - 1, 0)
    reach_frames = window[earlier]
    frame_of = jnp.arange(tail_rows) // TOK_FRAME
    open_cols = (frame_of >= BF - reach_frames) & (span_pos > 0)
    whole_key, whole_value = (
        lax.all_gather(own_key, "seq", axis=0, tiled=True),
        lax.all_gather(own_value, "seq", axis=0, tiled=True),
    )
    near_key, near_value = from_behind(
        (whole_key[-tail_rows:], whole_value[-tail_rows:]), "span", 1
    )
    usable = jnp.concatenate([jnp.ones((whole_key.shape[0],), bool), open_cols])
    attended = attend(
        own_query,
        jnp.concatenate([whole_key, near_key], 0),
        jnp.concatenate([whole_value, near_value], 0),
        usable,
        HEADS,
    )
    row_count = attended.shape[0]
    half_width = attended.shape[1] // 2
    swapped, gate_pair = (
        lax.all_to_all(attended, "section", split_axis=1, concat_axis=0, tiled=True),
        lax.all_to_all(
            gate_row.reshape(1, -1).astype(jnp.bfloat16),
            "section",
            split_axis=1,
            concat_axis=0,
            tiled=True,
        ).astype(jnp.float32),
    )
    own_latents = lax.dynamic_slice_in_dim(latents, section_pos * half_width, half_width, 1)
    after_one = (
        own_latents.astype(jnp.float32) + gate_pair[0] * swapped[:row_count].astype(jnp.float32)
    ).astype(jnp.bfloat16)
    second = (
        after_one.astype(jnp.float32) + gate_pair[1] * swapped[row_count:].astype(jnp.float32)
    ).astype(jnp.bfloat16)
    return finish_blend(second, intersection, blend_index, earlier, span_pos)


def solution(mesh):
    in_specs = (
        P(("span", "seq"), None),
        P("section", ("span", "seq"), None),
        P("section", ("span", "seq"), None),
        P("section", ("span", "seq"), None),
        P("section", None),
        P(),
        P(),
        P(),
    )
    out_specs = P("span", ("section", "seq"))
    return jax.shard_map(local, mesh=mesh, in_specs=in_specs, out_specs=out_specs, check_vma=False)
```

profile of v0, /device:TPU:4, one launch (start us, length us, event | category | flops | bytes accessed | tf_op | source)
XLA Modules:
  0.0 778.4 jit_solution(12352801000720409650)
XLA Ops:
  8.0 129.9 %all-gather.5.cloned.1.call-done = bf16[1,1008,5120]{2,1,0:T(8,128)(2,1)} async-done(((bf16[1,504,5120]{2,1,0:T(8,128)(2,1)}), bf16[1,1008,5120]{2,1,0:T(8,128)(2,1)}) %all-gather.5.cloned.1.call-update) | async-done | bytes 10321936 | tf_op jit(solution)/shard_map/all_gather | solution.py:89
  137.9 4.9 slice_bitcast_fusion.1
  144.9 122.3 %all-gather.7.cloned.1.call-done = bf16[1,1008,5120]{2,1,0:T(8,128)(2,1)} async-done(((bf16[1,504,5120]{2,1,0:T(8,128)(2,1)}), bf16[1,1008,5120]{2,1,0:T(8,128)(2,1)}) %all-gather.7.cloned.1.call-update) | async-done | bytes 10321936 | tf_op jit(solution)/shard_map/all_gather | solution.py:88
  267.2 4.9 slice_bitcast_fusion
  275.9 3.7 all-to-all-start
  279.6 7.9 %copy.24 = bf16[1,504,5120]{1,2,0:T(8,128)(2,1)} copy(bf16[1,504,5120]{2,1,0:T(8,128)(2,1)} %param.11) | data formatting | bytes 10321920 | tf_op args[1]
  288.9 14.9 %pad_maximum_fusion = bf16[1488,5120]{1,0:T(8,128)(2,1)} fusion(bf16[480,5120]{1,0:T(8,128)(2,1)} %collective-permute-done, bf16[1008,5120]{1,0:T(8,128)(2,1)} %bitcast.72), kind=kLoop, calls=%fused_computation.19 | loop fusion | flops 30474240 | bytes 30474240 | tf_op jit(solution)/shard_map/concatenate | solution.py:98
  303.8 27.1 %collective-permute-done.1 = bf16[480,5120]{1,0:T(8,128)(2,1)} collective-permute-done((bf16[480,5120]{1,0:T(8,128)(2,1)}, bf16[480,5120]{1,0:T(8,128)(2,1)}, u32[]{:S(2)}, u32[]{:S(2)}) %collective-permute-start.1) | collective-permute-done | bytes 4915232 | tf_op jit(solution)/shard_map/ppermute | solution.py:18
  330.9 9.4 %pad_maximum_fusion.1 = bf16[1488,5120]{1,0:T(8,128)(2,1)} fusion(bf16[480,5120]{1,0:T(8,128)(2,1)} %collective-permute-done.1, bf16[1008,5120]{1,0:T(8,128)(2,1)S(1)} %bitcast.75), kind=kLoop, calls=%fused_computation.20 | loop fusion | flops 30474240 | bytes 30474240 | tf_op jit(solution)/shard_map/concatenate | solution.py:97
  340.3 2.7 broadcast_in_dim.68
  342.9 236.2 %while.13 = (s32[]{:T(128)}, bf16[504,5120]{0,1:T(8,128)(2,1)}, bf16[1488,5120]{1,0:T(8,128)(2,1)}, pred[1488]{0:T(1024)(128)(4,1)S(1)}, bf16[504,5120]{0,1:T(8,...) while((s32[]{:T(128)}, bf16[504,5120]{0,1:T(8,128)(2,1)}, ...), condition=%wide.region_3.4_spmd, body=%wide.region_0.3_spmd.sunk | while | flops 1554160128 | bytes 43390316 | solution.py:54
  342.9 2.1 constant_dynamic-slice_fusion.5
  347.7 10.4 %fusion.38 = (f32[4,504]{1,0:T(4,128)S(1)}, f32[4,504,1488]{1,2,0:T(8,128)}) fusion(pred[1488]{0:T(1024)(128)(4,1)S(1)} %get-tuple-element.209, bf16[504,4,128]{0,2,1:T(8,128)(2,1)S(1)} %bitcast.80, bf16[1488,4,128]{0,2,1:T(8,128)(2,1)} %bitcast.70), kind=kOutput, calls=%fused_computation.57.clone.1 | convolution fusion | flops 779951616 | bytes 14048592 | tf_op jit(solution)/shard_map/while/body/eval_jaxpr/sub | solution.py:44
  358.8 6.7 fusion.39
  366.6 2.1 constant_dynamic-slice_fusion.5
  371.3 10.4 %fusion.38 = (f32[4,504]{1,0:T(4,128)S(1)}, f32[4,504,1488]{1,2,0:T(8,128)}) fusion(pred[1488]{0:T(1024)(128)(4,1)S(1)} %get-tuple-element.209, bf16[504,4,128]{0,2,1:T(8,128)(2,1)S(1)} %bitcast.80, bf16[1488,4,128]{0,2,1:T(8,128)(2,1)} %bitcast.70), kind=kOutput, calls=%fused_computation.57.clone.1 | convolution fusion | flops 779951616 | bytes 14048592 | tf_op jit(solution)/shard_map/while/body/eval_jaxpr/sub | solution.py:44
  382.4 6.7 fusion.39
  390.2 2.1 constant_dynamic-slice_fusion.5
  394.9 10.4 %fusion.38 = (f32[4,504]{1,0:T(4,128)S(1)}, f32[4,504,1488]{1,2,0:T(8,128)}) fusion(pred[1488]{0:T(1024)(128)(4,1)S(1)} %get-tuple-element.209, bf16[504,4,128]{0,2,1:T(8,128)(2,1)S(1)} %bitcast.80, bf16[1488,4,128]{0,2,1:T(8,128)(2,1)} %bitcast.70), kind=kOutput, calls=%fused_computation.57.clone.1 | convolution fusion | flops 779951616 | bytes 14048592 | tf_op jit(solution)/shard_map/while/body/eval_jaxpr/sub | solution.py:44
  406.0 6.7 fusion.39
  413.8 2.1 constant_dynamic-slice_fusion.5
  418.5 10.4 %fusion.38 = (f32[4,504]{1,0:T(4,128)S(1)}, f32[4,504,1488]{1,2,0:T(8,128)}) fusion(pred[1488]{0:T(1024)(128)(4,1)S(1)} %get-tuple-element.209, bf16[504,4,128]{0,2,1:T(8,128)(2,1)S(1)} %bitcast.80, bf16[1488,4,128]{0,2,1:T(8,128)(2,1)} %bitcast.70), kind=kOutput, calls=%fused_computation.57.clone.1 | convolution fusion | flops 779951616 | bytes 14048592 | tf_op jit(solution)/shard_map/while/body/eval_jaxpr/sub | solution.py:44
  429.6 6.7 fusion.39
  437.4 2.1 constant_dynamic-slice_fusion.5
  442.1 10.4 %fusion.38 = (f32[4,504]{1,0:T(4,128)S(1)}, f32[4,504,1488]{1,2,0:T(8,128)}) fusion(pred[1488]{0:T(1024)(128)(4,1)S(1)} %get-tuple-element.209, bf16[504,4,128]{0,2,1:T(8,128)(2,1)S(1)} %bitcast.80, bf16[1488,4,128]{0,2,1:T(8,128)(2,1)} %bitcast.70), kind=kOutput, calls=%fused_computation.57.clone.1 | convolution fusion | flops 779951616 | bytes 14048592 | tf_op jit(solution)/shard_map/while/body/eval_jaxpr/sub | solution.py:44
  453.3 6.7 fusion.39
  465.7 10.4 %fusion.38 = (f32[4,504]{1,0:T(4,128)S(1)}, f32[4,504,1488]{1,2,0:T(8,128)}) fusion(pred[1488]{0:T(1024)(128)(4,1)S(1)} %get-tuple-element.209, bf16[504,4,128]{0,2,1:T(8,128)(2,1)S(1)} %bitcast.80, bf16[1488,4,128]{0,2,1:T(8,128)(2,1)} %bitcast.70), kind=kOutput, calls=%fused_computation.57.clone.1 | convolution fusion | flops 779951616 | bytes 14048592 | tf_op jit(solution)/shard_map/while/body/eval_jaxpr/sub | solution.py:44
  476.9 6.7 fusion.39
  484.6 2.1 constant_dynamic-slice_fusion.5
  489.4 10.4 %fusion.38 = (f32[4,504]{1,0:T(4,128)S(1)}, f32[4,504,1488]{1,2,0:T(8,128)}) fusion(pred[1488]{0:T(1024)(128)(4,1)S(1)} %get-tuple-element.209, bf16[504,4,128]{0,2,1:T(8,128)(2,1)S(1)} %bitcast.80, bf16[1488,4,128]{0,2,1:T(8,128)(2,1)} %bitcast.70), kind=kOutput, calls=%fused_computation.57.clone.1 | convolution fusion | flops 779951616 | bytes 14048592 | tf_op jit(solution)/shard_map/while/body/eval_jaxpr/sub | solution.py:44
  500.5 6.7 fusion.39
  508.2 2.1 constant_dynamic-slice_fusion.5
  513.0 10.4 %fusion.38 = (f32[4,504]{1,0:T(4,128)S(1)}, f32[4,504,1488]{1,2,0:T(8,128)}) fusion(pred[1488]{0:T(1024)(128)(4,1)S(1)} %get-tuple-element.209, bf16[504,4,128]{0,2,1:T(8,128)(2,1)S(1)} %bitcast.80, bf16[1488,4,128]{0,2,1:T(8,128)(2,1)} %bitcast.70), kind=kOutput, calls=%fused_computation.57.clone.1 | convolution fusion | flops 779951616 | bytes 14048592 | tf_op jit(solution)/shard_map/while/body/eval_jaxpr/sub | solution.py:44
  524.1 6.7 fusion.39
  531.9 2.1 constant_dynamic-slice_fusion.5
  536.6 10.4 %fusion.38 = (f32[4,504]{1,0:T(4,128)S(1)}, f32[4,504,1488]{1,2,0:T(8,128)}) fusion(pred[1488]{0:T(1024)(128)(4,1)S(1)} %get-tuple-element.209, bf16[504,4,128]{0,2,1:T(8,128)(2,1)S(1)} %bitcast.80, bf16[1488,4,128]{0,2,1:T(8,128)(2,1)} %bitcast.70), kind=kOutput, calls=%fused_computation.57.clone.1 | convolution fusion | flops 779951616 | bytes 14048592 | tf_op jit(solution)/shard_map/while/body/eval_jaxpr/sub | solution.py:44
  547.7 6.7 fusion.39
  555.5 2.1 constant_dynamic-slice_fusion.5
  560.2 10.4 %fusion.38 = (f32[4,504]{1,0:T(4,128)S(1)}, f32[4,504,1488]{1,2,0:T(8,128)}) fusion(pred[1488]{0:T(1024)(128)(4,1)S(1)} %get-tuple-element.209, bf16[504,4,128]{0,2,1:T(8,128)(2,1)S(1)} %bitcast.80, bf16[1488,4,128]{0,2,1:T(8,128)(2,1)} %bitcast.70), kind=kOutput, calls=%fused_computation.57.clone.1 | convolution fusion | flops 779951616 | bytes 14048592 | tf_op jit(solution)/shard_map/while/body/eval_jaxpr/sub | solution.py:44
  571.4 6.7 fusion.39
  579.2 7.8 copy.27
  586.9 6.1 all-to-all-start.1
  593.2 112.3 %all-to-all-done.1 = bf16[504,2,2560]{2,0,1:T(8,128)(2,1)} async-done(((bf16[504,2,2560]{2,0,1:T(8,128)(2,1)}), bf16[504,2,2560]{2,0,1:T(8,128)(2,1)}, u32[]{:S(2)}, u32[]{:S(2)}) %all-to-all-start.1) | async-done | bytes 5160992 | tf_op jit(solution)/shard_map/all_to_all | solution.py:105
  705.4 4.5 fusion.13
  710.2 33.0 %all_to_all.48 = bf16[504,2,1280]{2,0,1:T(8,128)(2,1)S(1)} all-to-all(bf16[504,2,1280]{2,0,1:T(8,128)(2,1)S(1)} %bitcast.83), channel_id=1, replica_groups=mesh['section'=2,'span'=8,'seq'=2] {'seq'}, dimensions={1} | all-to-all | bytes 5160960 | tf_op jit(solution)/shard_map/all_to_all | solution.py:59
  750.7 12.9 %collective-permute-done.2 = bf16[480,1280]{1,0:T(8,128)(2,1)} collective-permute-done((bf16[480,1280]{1,0:T(8,128)(2,1)}, bf16[480,1280]{1,0:T(8,128)(2,1)}, u32[]{:S(2)}, u32[]{:S(2)}) %collective-permute-start.2) | collective-permute-done | bytes 1228832 | tf_op jit(solution)/shard_map/ppermute | solution.py:18
  763.6 3.0 gather_fusion
  768.6 3.0 pad_maximum_fusion.2
  (101 shorter events, 63.1 us)
Async XLA Ops:
  6.5 131.3 %all-gather.5.cloned.1.call-start = ((), (), s32[]{:S(2)}) async-start(), calls=%async_computation.3 | async-start | bytes 15482880 | tf_op jit(solution)/shard_map/all_gather | solution.py:89
  7.3 259.9 %all-gather.7.cloned.1.call-start = ((), (), s32[]{:S(2)}) async-start(), calls=%async_computation.4 | async-start | bytes 15482880 | tf_op jit(solution)/shard_map/all_gather | solution.py:88
  142.8 131.2 %copy-start = (f32[1,5120]{1,0:T(1,128)S(1)}, f32[1,5120]{1,0:T(1,128)}, u32[]{:S(2)}) copy-start(f32[1,5120]{1,0:T(1,128)} %param.14) | copy-start | bytes 61444
  142.8 146.0 %collective-permute-start = (bf16[480,5120]{1,0:T(8,128)(2,1)}, bf16[480,5120]{1,0:T(8,128)(2,1)}, u32[]{:S(2)}, u32[]{:S(2)}) collective-permute-start(bf16[480,5120]{1,0:T(8,128)(2,1)} %slice_bitcast_fusion.1), channel_id=1, source_target_pairs={{0,2},{2,4},{4,6},{6,8},{8,10},{10,12},{12,14},{1,3},{3,5},{5,7},{... | collective-permute-start | bytes 14745608 | tf_op jit(solution)/shard_map/ppermute | solution.py:18
  272.1 58.8 %collective-permute-start.1 = (bf16[480,5120]{1,0:T(8,128)(2,1)}, bf16[480,5120]{1,0:T(8,128)(2,1)}, u32[]{:S(2)}, u32[]{:S(2)}) collective-permute-start(bf16[480,5120]{1,0:T(8,128)(2,1)} %slice_bitcast_fusion), channel_id=1, source_target_pairs={{0,2},{2,4},{4,6},{6,8},{8,10},{10,12},{12,14},{1,3},{3,5},{5,7},{... | collective-permute-start | bytes 14745608 | tf_op jit(solution)/shard_map/ppermute | solution.py:18
  275.9 311.0 %all-to-all-start = ((bf16[2,2,1280]{2,1,0:T(2,128)(2,1)}), bf16[2,2,1280]{2,1,0:T(2,128)(2,1)S(1)}, u32[]{:S(2)}, u32[]{:S(2)}) async-start(bf16[2,2,1280]{2,1,0:T(2,128)(2,1)} %reshape.129), calls=%async_computation | async-start | bytes 20480 | tf_op jit(solution)/shard_map/all_to_all | solution.py:106
  279.6 7.9 %copy-start.1 = (s32[7]{0:T(128)S(1)}, s32[7]{0:T(128)}, u32[]{:S(2)}) copy-start(s32[7]{0:T(128)} %param.15) | copy-start | bytes 88
  288.9 42.0 %slice-start = ((s8[10321920]{0:T(1024)(128)(4,1)}), s8[4194304]{0:T(1024)(128)(4,1)S(1)}, s32[]{:S(2)}) async-start(s8[10321920]{0:T(1024)(128)(4,1)} %bitcast.73), calls=%async_computation.5 | async-start | bytes 8388608
  288.9 42.0 %slice-start.1 = ((s8[10321920]{0:T(1024)(128)(4,1)}), s8[4194304]{0:T(1024)(128)(4,1)S(1)}, s32[]{:S(2)}) async-start(s8[10321920]{0:T(1024)(128)(4,1)} %bitcast.73), calls=%async_computation.6 | async-start | bytes 8388608
  288.9 42.0 %slice-start.2 = ((s8[10321920]{0:T(1024)(128)(4,1)}), s8[1933312]{0:T(1024)(128)(4,1)S(1)}, s32[]{:S(2)}) async-start(s8[10321920]{0:T(1024)(128)(4,1)} %bitcast.73), calls=%async_computation.7 | async-start | bytes 3866624
  586.9 118.5 %all-to-all-start.1 = ((bf16[504,2,2560]{2,0,1:T(8,128)(2,1)}), bf16[504,2,2560]{2,0,1:T(8,128)(2,1)}, u32[]{:S(2)}, u32[]{:S(2)}) async-start(bf16[504,2,2560]{2,0,1:T(8,128)(2,1)} %copy.27), calls=%async_computation.1 | async-start | bytes 10321920 | tf_op jit(solution)/shard_map/all_to_all | solution.py:105
  710.0 36.3 %copy-start.2 = (s32[7]{0:T(128)S(1)}, s32[7]{0:T(128)}, u32[]{:S(2)}) copy-start(s32[7]{0:T(128)} %param.16) | copy-start | bytes 88
  744.3 19.3 %collective-permute-start.2 = (bf16[480,1280]{1,0:T(8,128)(2,1)}, bf16[480,1280]{1,0:T(8,128)(2,1)}, u32[]{:S(2)}, u32[]{:S(2)}) collective-permute-start(bf16[480,1280]{1,0:T(8,128)(2,1)} %slice.51), channel_id=1, source_target_pairs={{0,2},{2,4},{4,6},{6,8},{8,10},{10,12},{12,14},{1,3},{3,5},{5,7},{... | collective-permute-start | bytes 3686408 | tf_op jit(solution)/shard_map/ppermute | solution.py:18
Sparse Core Ops, SparseCore 0:
  8.9 128.9 all-gather.4
  139.4 127.7 all-gather.6
where the time goes:
time: 781 us; the launch traced here: 778 us
  waiting for transfers between devices  406 us (52%)
  matrix products  171 us (22%)
  local copies, waits for them, and re-layouts  101 us (13%)
  other arithmetic  36 us (5%)
  blocking collectives  33 us (4%)
  starting transfers between devices  15.7 us (2%)
  between operations  14.9 us (2%)
    all_gather x1, waiting for transfers between devices, local(): lax.all_gather(own_value, 'seq', axis=0, tiled=True)  130 us
    all_gather x1, waiting for transfers between devices, local(): lax.all_gather(own_key, 'seq', axis=0, tiled=True)  122 us
    all_to_all x1, waiting for transfers between devices, local(): lax.all_to_all(attended, 'section', split_axis=1, concat_axis=0, tiled=True)  112 us
    sub x10, matrix products, head_block(): lifted = jnp.exp(scores - row_max)  104 us
    dot_general x10, matrix products, head_block(): jnp.einsum('hqk,khd->qhd', weights, value_part, preferred_element_type=jn...  66.9 us
    ppermute x3, waiting for transfers between devices, from_behind(): return lax.ppermute(shard, axis, pairs)  39.9 us
    dynamic_slice x20, local copies, waits for them, and re-layouts, head_block(): lax.dynamic_slice_in_dim(key_block, offset, group_width, 1)  36.3 us
    all_to_all x1, blocking collectives, finish_blend(): lax.all_to_all(second, 'seq', split_axis=1, concat_axis=0, tiled=True)  33 us
  transfers between devices with their start and end apart: 7, of which 5 were waited for; matrix products, arithmetic and copies ran while one was open for 38% of the time, Pallas kernels for 0%

commit v1 on v0

v1 whole, which is shorter than its diff:
```python
import functools
import math

import jax
import jax.numpy as jnp
from jax import lax
from jax.experimental import pallas as pl
from jax.experimental.pallas import tpu as pltpu
from jax.sharding import PartitionSpec as P

HEAD_DIM = 128
TOK_FRAME = 48
BF = 10
WEIGHTS = 8
SUBS = 2
CHUNKS = 2 * SUBS
MESH = pl.DeviceIdType.MESH


def kernel(
    spans,
    lat_hbm, q_hbm, k_hbm, v_hbm, gate_ref, window_ref,
    second, prev,
    q_buf, k_buf, v_buf, near_k, near_v, att, att_recv, lat, gate_recv, v_ext, k_mask,
    own_sem, lat_sem, seq_send, seq_recv, lat_send, lat_recv, near_send, near_recv,
    sect_send, sect_recv, gate_send, gate_recv_sem, tail_send, tail_recv,
):
    s = lax.axis_index("section")
    c = lax.axis_index("span")
    q = lax.axis_index("seq")
    rows, width = lat_hbm.shape
    quarter = width // 4
    part = quarter // SUBS
    heads = part // HEAD_DIM
    tail_rows = BF * TOK_FRAME
    has_prev = c > 0
    has_next = c < spans - 1
    to_seq = {"seq": 1 - q}
    to_sect = {"section": 1 - s}
    to_next = {"span": jnp.minimum(c + 1, spans - 1)}
    inputs = (k_hbm, v_hbm, q_hbm)
    bufs = (k_buf, v_buf, q_buf)
    nears = (near_k, near_v)

    def columns(j, who):
        t = 1 - s if j < SUBS else s
        return pl.ds(pl.multiple_of((2 * t + who) * quarter + (j % SUBS) * part, 128), part)

    def own_copy(j, i):
        return pltpu.make_async_copy(
            inputs[i].at[0, :, columns(j, q)], bufs[i].at[j, 0], own_sem.at[j, i]
        )

    def seq_copy(j, i):
        return pltpu.make_async_remote_copy(
            src_ref=inputs[i].at[0, :, columns(j, 1 - q)], dst_ref=bufs[i].at[j, 1],
            send_sem=seq_send.at[j, i], recv_sem=seq_recv.at[j, i],
            device_id=to_seq, device_id_type=MESH,
        )

    def near_copy(j, i, straight):
        source = inputs[i].at[0, :, columns(j, q)] if straight else bufs[i].at[j, 1]
        return pltpu.make_async_remote_copy(
            src_ref=source, dst_ref=nears[i].at[j],
            send_sem=near_send.at[j, i], recv_sem=near_recv.at[j, i],
            device_id=to_next, device_id_type=MESH,
        )

    def sect_copy(j):
        return pltpu.make_async_remote_copy(
            src_ref=att.at[j], dst_ref=att_recv.at[j],
            send_sem=sect_send.at[j], recv_sem=sect_recv.at[j],
            device_id=to_sect, device_id_type=MESH,
        )

    def lat_own(jj):
        return pltpu.make_async_copy(
            lat_hbm.at[:, columns(SUBS + jj, q)], lat.at[jj, 0], lat_sem.at[jj]
        )

    def lat_copy(jj):
        return pltpu.make_async_remote_copy(
            src_ref=lat_hbm.at[:, columns(SUBS + jj, 1 - q)], dst_ref=lat.at[jj, 1],
            send_sem=lat_send.at[jj], recv_sem=lat_recv.at[jj],
            device_id=to_seq, device_id_type=MESH,
        )

    gate_copy = pltpu.make_async_remote_copy(
        src_ref=gate_ref, dst_ref=gate_recv, send_sem=gate_send.at[0],
        recv_sem=gate_recv_sem.at[0], device_id=to_sect, device_id_type=MESH,
    )

    def tail_copy(jj):
        piece = pl.ds(jj * part, part)
        return pltpu.make_async_remote_copy(
            src_ref=second.at[1, :, piece], dst_ref=prev.at[:, piece],
            send_sem=tail_send.at[jj], recv_sem=tail_recv.at[jj],
            device_id=to_next, device_id_type=MESH,
        )

    barrier = pltpu.get_barrier_semaphore()
    pl.semaphore_signal(barrier, inc=1, device_id=to_seq, device_id_type=MESH)
    pl.semaphore_signal(barrier, inc=1, device_id=to_sect, device_id_type=MESH)

    @pl.when(has_next)
    def _():
        pl.semaphore_signal(barrier, inc=1, device_id=to_next, device_id_type=MESH)

    @pl.when(has_prev)
    def _():
        pl.semaphore_signal(
            barrier, inc=1, device_id={"span": jnp.maximum(c - 1, 0)}, device_id_type=MESH
        )

    neighbours = 2 + jnp.where(has_next, 1, 0) + jnp.where(has_prev, 1, 0)
    pl.semaphore_wait(barrier, neighbours)

    for i in range(3):
        seq_copy(0, i).start()

    def straight_near(j):
        @pl.when(has_next & (q == 1))
        def _():
            for i in range(2):
                near_copy(j, i, True).start()

    straight_near(0)
    gate_copy.start()
    for j in range(CHUNKS):
        for i in range(3):
            own_copy(j, i).start()
    for jj in range(SUBS):
        lat_own(jj).start()

    reach = jnp.where(has_prev, window_ref[jnp.maximum(c - 1, 0)], 0)
    first_open = rows - reach * TOK_FRAME
    open_rows = lax.broadcasted_iota(jnp.int32, (rows, HEAD_DIM), 0) >= first_open
    ones = jnp.ones((rows, HEAD_DIM), jnp.bfloat16)
    v_ext[0, :, HEAD_DIM:] = ones
    v_ext[1, :, HEAD_DIM:] = ones
    v_ext[2, :, HEAD_DIM:] = jnp.where(open_rows, 1.0, 0.0).astype(jnp.bfloat16)

    @pl.when(jnp.logical_not(has_prev))
    def _():
        near_k[...] = jnp.zeros_like(near_k)
        near_v[...] = jnp.zeros_like(near_v)
        prev[...] = jnp.zeros_like(prev)

    factor = math.log2(math.e) / math.sqrt(HEAD_DIM)

    def attend(j):
        def one_head(head, carry):
            lanes = pl.ds(pl.multiple_of(head * HEAD_DIM, HEAD_DIM), HEAD_DIM)
            open_now = lax.broadcasted_iota(jnp.int32, (rows, HEAD_DIM), 0) >= first_open
            key_own = k_buf[j, 0, :, lanes]
            spare = key_own[:8].astype(jnp.float32)[:1]
            k_mask[...] = jnp.where(
                open_now, near_k[j, :, lanes].astype(jnp.float32), spare
            ).astype(jnp.bfloat16)
            v_ext[0, :, :HEAD_DIM] = v_buf[j, 0, :, lanes]
            v_ext[1, :, :HEAD_DIM] = v_buf[j, 1, :, lanes]
            v_ext[2, :, :HEAD_DIM] = jnp.where(
                open_now, near_v[j, :, lanes].astype(jnp.float32), 0.0
            ).astype(jnp.bfloat16)

            def one_side(who, carry):
                query = q_buf[j, who, :, lanes]
                keys = (k_buf[j, 0, :, lanes], k_buf[j, 1, :, lanes], k_mask[...])
                scores = [
                    lax.dot_general(
                        query, key, (((1,), (1,)), ((), ())), preferred_element_type=jnp.float32
                    )
                    for key in keys
                ]
                top = functools.reduce(
                    jnp.maximum, [jnp.max(x, axis=-1, keepdims=True) for x in scores]
                )
                total = None
                for n, x in enumerate(scores):
                    lifted = jnp.exp2((x - top) * factor).astype(jnp.bfloat16)
                    term = jnp.dot(lifted, v_ext[n], preferred_element_type=jnp.float32)
                    total = term if total is None else total + term
                result = total[:, :HEAD_DIM] / total[:, HEAD_DIM:]
                att[j, lax.rem(who + q, 2), :, lanes] = result.astype(jnp.bfloat16)
                return carry

            return lax.fori_loop(0, 2, one_side, carry)

        lax.fori_loop(0, heads, one_head, 0)

    for j in range(CHUNKS):
        for i in range(3):
            seq_copy(j, i).wait_recv()
            if j + 1 < CHUNKS:
                seq_copy(j + 1, i).start()
            if i < 2:
                @pl.when(has_next & (q == 0))
                def _():
                    near_copy(j, i, False).start()
        if j + 1 < CHUNKS:
            straight_near(j + 1)
        if j >= SUBS:
            lat_copy(j - SUBS).start()
        for i in range(3):
            own_copy(j, i).wait()

        @pl.when(has_prev)
        def _():
            for i in range(2):
                near_copy(j, i, False).wait_recv()

        attend(j)
        if j < SUBS:
            sect_copy(j).start()

    gate_copy.wait_recv()
    for jj in range(SUBS):
        lat_own(jj).wait()
        lat_copy(jj).wait_recv()
        sect_copy(jj).wait_recv()

        def finish(block, carry):
            side, lane_block = lax.rem(block, 2), block // 2
            at = pl.multiple_of(lane_block * HEAD_DIM, HEAD_DIM)
            lanes = pl.ds(at, HEAD_DIM)
            place = pl.ds(
                pl.multiple_of((2 * s + q) * quarter + jj * part + at, HEAD_DIM), HEAD_DIM
            )
            gate_own, gate_other = gate_ref[:, place], gate_recv[:, place]
            mine = att[SUBS + jj, side, :, lanes].astype(jnp.float32)
            other = att_recv[jj, side, :, lanes].astype(jnp.float32)
            gated_own, gated_other = gate_own * mine, gate_other * other
            first = jnp.where(s == 0, gated_own, gated_other)
            later = jnp.where(s == 0, gated_other, gated_own)
            base = lat[jj, lax.rem(side + q, 2), :, lanes].astype(jnp.float32)
            after_one = (base + first).astype(jnp.bfloat16)
            result = (after_one.astype(jnp.float32) + later).astype(jnp.bfloat16)
            second[side, :, pl.ds(pl.multiple_of(jj * part + at, HEAD_DIM), HEAD_DIM)] = result
            return carry

        lax.fori_loop(0, 2 * heads, finish, 0)

        @pl.when(has_next)
        def _():
            tail_copy(jj).start()

    for jj in range(SUBS):
        @pl.when(has_prev)
        def _():
            tail_copy(jj).wait_recv()

        @pl.when(has_next)
        def _():
            tail_copy(jj).wait_send()

        sect_copy(jj).wait_send()
        lat_copy(jj).wait_send()
    gate_copy.wait_send()
    for j in range(CHUNKS):
        for i in range(3):
            seq_copy(j, i).wait_send()

        @pl.when(has_next)
        def _():
            for i in range(2):
                near_copy(j, i, False).wait_send()


def local(
    latents, queries, key_states, value_states, gate_scales, window, intersection, blend_index
):
    rows, width = latents.shape
    quarter = width // 4
    part = quarter // SUBS
    spans = lax.axis_size("span")
    span_pos = lax.axis_index("span")
    tail_rows = BF * TOK_FRAME
    wide = jnp.bfloat16
    dma = pltpu.SemaphoreType.DMA
    flops = 4 * 2 * rows * 3 * rows * width // 2
    second, prev = pl.pallas_call(
        functools.partial(kernel, spans),
        out_shape=(
            jax.ShapeDtypeStruct((2, rows, quarter), wide),
            jax.ShapeDtypeStruct((rows, quarter), wide),
        ),
        in_specs=[pl.BlockSpec(memory_space=pl.ANY)] * 4
        + [pl.BlockSpec(memory_space=pltpu.VMEM), pl.BlockSpec(memory_space=pltpu.SMEM)],
        out_specs=(pl.BlockSpec(memory_space=pltpu.VMEM),) * 2,
        scratch_shapes=[
            pltpu.VMEM((CHUNKS, 2, rows, part), wide),
            pltpu.VMEM((CHUNKS, 2, rows, part), wide),
            pltpu.VMEM((CHUNKS, 2, rows, part), wide),
            pltpu.VMEM((CHUNKS, rows, part), wide),
            pltpu.VMEM((CHUNKS, rows, part), wide),
            pltpu.VMEM((CHUNKS, 2, rows, part), wide),
            pltpu.VMEM((SUBS, 2, rows, part), wide),
            pltpu.VMEM((SUBS, 2, rows, part), wide),
            pltpu.VMEM(gate_scales.shape, jnp.float32),
            pltpu.VMEM((3, rows, 2 * HEAD_DIM), wide),
            pltpu.VMEM((rows, HEAD_DIM), wide),
            dma((CHUNKS, 3)), dma((SUBS,)), dma((CHUNKS, 3)), dma((CHUNKS, 3)),
            dma((SUBS,)), dma((SUBS,)), dma((CHUNKS, 2)), dma((CHUNKS, 2)),
            dma((SUBS,)), dma((SUBS,)), dma((1,)), dma((1,)), dma((SUBS,)), dma((SUBS,)),
        ],
        cost_estimate=pl.CostEstimate(
            flops=flops, bytes_accessed=8 * rows * width, transcendentals=flops // 512
        ),
        compiler_params=pltpu.CompilerParams(
            collective_id=0, has_side_effects=True, vmem_limit_bytes=60 * 1024 * 1024
        ),
    )(latents, queries, key_states, value_states, gate_scales, window)

    earlier = jnp.maximum(span_pos - 1, 0)
    whole = second.reshape(2 * rows, quarter)
    previous = prev[rows - tail_rows:].reshape(BF, TOK_FRAME, quarter)
    length = intersection[earlier]
    frame_ids = jnp.arange(BF)
    source = jnp.clip(BF - length + frame_ids, 0, BF - 1)
    picked = jnp.take(previous, source, axis=0).astype(jnp.float32)
    weight = ((blend_index[earlier].astype(jnp.float32) + 0.5) / WEIGHTS)[:, None, None]
    active = (frame_ids < length) & (span_pos > 0)
    leading = whole[:tail_rows].reshape(BF, TOK_FRAME, quarter).astype(jnp.float32)
    blended = jnp.where(active[:, None, None], weight * leading + (1.0 - weight) * picked, leading)
    blended = blended.astype(wide).reshape(tail_rows, quarter)
    return jnp.concatenate([blended, whole[tail_rows:]], 0)


def solution(mesh):
    in_specs = (
        P(("span", "seq"), None),
        P("section", ("span", "seq"), None),
        P("section", ("span", "seq"), None),
        P("section", ("span", "seq"), None),
        P("section", None),
        P(),
        P(),
        P(),
    )
    out_specs = P("span", ("section", "seq"))
    return jax.shard_map(local, mesh=mesh, in_specs=in_specs, out_specs=out_specs, check_vma=False)
```

time: 781 us -> 277 us (0.35)
  waiting for transfers between devices: 406 us -> 0 us
  Pallas kernels: 0 us -> 267 us
  matrix products: 171 us -> 0 us
  local copies, waits for them, and re-layouts: 101 us -> 3.95 us
  blocking collectives: 33 us -> 0 us
  other arithmetic: 36 us -> 5.2 us
  starting transfers between devices: 15.7 us -> 0 us
  between operations: 14.9 us -> 0.73 us
    pallas_call x0 -> x1, Pallas kernels: none -> 267 us  [local(): pl.pallas_call(functools.partial(kernel, spans), out_shape=(jax.ShapeDtyp...]
    all_gather x2 -> x0, waiting for transfers between devices: 252 us -> none  [the longest x1 130 us: local(): lax.all_gather(own_value, 'seq', axis=0, tiled=True)]
    all_to_all x2 -> x0, waiting for transfers between devices: 112 us -> none  [the longest x1 112 us: local(): lax.all_to_all(attended, 'section', split_axis=1, concat_axis=0, tiled=True)]
    sub x10 -> x0, matrix products: 104 us -> none  [head_block(): lifted = jnp.exp(scores - row_max)]
    dot_general x10 -> x0, matrix products: 66.9 us -> none  [head_block(): jnp.einsum('hqk,khd->qhd', weights, value_part, preferred_element_type=jn...]
    dynamic_slice x42 -> x1, local copies, waits for them, and re-layouts: 55.1 us -> 1.24 us  [local(): length = intersection[earlier]]
    ppermute x3 -> x0, waiting for transfers between devices: 39.9 us -> none  [from_behind(): return lax.ppermute(shard, axis, pairs)]
    all_to_all x1 -> x0, blocking collectives: 33 us -> none  [finish_blend(): lax.all_to_all(second, 'seq', split_axis=1, concat_axis=0, tiled=True)]
  transfers between devices with their start and end apart: 7 -> 0, of which waited for: 5 -> 0; matrix products, arithmetic and copies ran while one was open for 38% -> 0% of each run, Pallas kernels for 0% -> 0%
where the time goes in v1:
time: 277 us
  Pallas kernels  267 us (96%)
  other arithmetic  5.2 us (2%)
  local copies, waits for them, and re-layouts  3.95 us (1%)
    pallas_call x1, Pallas kernels, local(): pl.pallas_call(functools.partial(kernel, spans), out_shape=(jax.ShapeDtyp...  267 us

profile of v1, /device:TPU:4, one launch (start us, length us, event | category | flops | bytes accessed | tf_op | source)
XLA Modules:
  0.0 276.9 jit_solution(6750469531313354866)
XLA Ops:
  0.0 1.2 dynamic_slice.6
  1.9 0.7 compare_and_fusion.1
  2.6 0.7 broadcast_subtract_fusion
  3.3 0.1 broadcast_in_dim.31
  3.4 0.1 broadcast_in_dim.32
  3.4 0.1 broadcast_in_dim.28
  3.5 0.1 broadcast_in_dim.29
  3.6 0.1 mul.30
  3.7 0.1 mul.31
  3.8 0.1 mul.26
  3.9 0.1 mul.27
  3.9 267.0 %shard_map.82 = (bf16[2,504,1280]{2,1,0:T(8,128)(2,1)}, bf16[504,1280]{1,0:T(8,128)(2,1)}) custom-call(bf16[504,5120]{1,0:T(8,128)(2,1)} %lat_hbm.1, bf16[1,504,5120]{2,1,0:T(8,128)(2,1)} %q_hbm.1, bf16[1,504,5120]{2,1,0:T(8,128)(2,1)} %k_hbm.1, bf16[1,504,5120]{2,1,0:T(8,128)(2,1)} %v_hbm.1, f32[1,5120]{1,0:T(1,128)} %gate_ref.1, s32[7]{0:T(128)} %window_ref.1), custom_call_target="tpu_custom_call" | custom-call | flops 15606743040 | bytes 20643840 | tf_op jit(solution)/shard_map/pallas_call | solution.py:281
  271.0 1.4 slice.10
  272.4 0.6 gather_fusion
  273.0 0.0 copy-start
  273.0 2.2 fusion.1
  275.2 0.0 copy-done
  275.2 0.1 slice.15
  275.3 1.6 pad_maximum_fusion
  (3 shorter events, 0.0 us)
Async XLA Ops:
  273.0 2.2 copy-start

commit v2 on v1

v2 whole, which is shorter than its diff:
```python
import functools
import math

import jax
import jax.numpy as jnp
from jax import lax
from jax.experimental import pallas as pl
from jax.experimental.pallas import tpu as pltpu
from jax.sharding import PartitionSpec as P

HEAD_DIM = 128
TOK_FRAME = 48
BF = 10
WEIGHTS = 8
SLOTS = 6
SHARED = 2
LAST = SLOTS - 1
MESH = pl.DeviceIdType.MESH


def kernel(
    spans,
    lat_hbm, q_hbm, k_hbm, v_hbm, gate_ref, window_ref,
    second, prev,
    q_buf, k_buf, v_buf, near_k, near_v, att_far, att_own, att_recv, lat, tail,
    gate_recv, v_ext, k_mask,
    own_sem, lat_sem, seq_send, seq_recv, lat_send, lat_recv, near_send, near_recv,
    sect_send, sect_recv, gate_send, gate_recv_sem, tail_send, tail_recv,
):
    s = lax.axis_index("section")
    c = lax.axis_index("span")
    q = lax.axis_index("seq")
    rows, width = lat_hbm.shape
    quarter = width // 4
    part = q_buf.shape[3]
    rest = quarter - 2 * part
    tail_rows = BF * TOK_FRAME
    has_prev = c > 0
    has_next = c < spans - 1
    inner = q != s
    outer = q == s
    to_seq = {"seq": 1 - q}
    to_sect = {"section": 1 - s}
    to_cross = {"section": 1 - s, "seq": 1 - q}
    to_next = {"span": jnp.minimum(c + 1, spans - 1)}
    inputs = (k_hbm, v_hbm, q_hbm)
    bufs = (k_buf, v_buf, q_buf)
    nears = (near_k, near_v)

    def breadth(n):
        return rest if n == LAST else part

    def columns(n, who):
        if n < SHARED:
            first = (1 - s) * 2 * quarter + who * (quarter + rest) + n * part
        elif n == SHARED:
            first = (1 - s) * 2 * quarter + 2 * part
        else:
            first = (2 * s + who) * quarter + (n - 3) * part
        return pl.ds(pl.multiple_of(first, HEAD_DIM), breadth(n))

    def place(ref, n, who):
        return ref.at[n, who, :, pl.ds(0, breadth(n))]

    def own_copy(n, i):
        return pltpu.make_async_copy(
            inputs[i].at[0, :, columns(n, q)], place(bufs[i], n, 0), own_sem.at[n, i]
        )

    def seq_copy(n, i):
        return pltpu.make_async_remote_copy(
            src_ref=inputs[i].at[0, :, columns(n, 1 - q)], dst_ref=place(bufs[i], n, 1),
            send_sem=seq_send.at[n, i], recv_sem=seq_recv.at[n, i],
            device_id=to_seq, device_id_type=MESH,
        )

    def near_copy(n, i, straight):
        source = inputs[i].at[0, :, columns(n, q)] if straight else place(bufs[i], n, 1)
        return pltpu.make_async_remote_copy(
            src_ref=source, dst_ref=nears[i].at[n, :, pl.ds(0, breadth(n))],
            send_sem=near_send.at[n, i], recv_sem=near_recv.at[n, i],
            device_id=to_next, device_id_type=MESH,
        )

    def sect_copy(n):
        at = pl.multiple_of(q * rest + n * part, HEAD_DIM)
        return pltpu.make_async_remote_copy(
            src_ref=att_far.at[n], dst_ref=att_recv.at[:, :, pl.ds(at, part)],
            send_sem=sect_send.at[n], recv_sem=sect_recv.at[n],
            device_id=to_sect, device_id_type=MESH,
        )

    def shared_copy(cross):
        whose = 1 - q if cross else q
        source = pl.ds(pl.multiple_of(whose * rest, HEAD_DIM), rest)
        target = pl.ds(pl.multiple_of((1 - whose) * 2 * part, HEAD_DIM), rest)
        return pltpu.make_async_remote_copy(
            src_ref=att_far.at[SHARED, :, :, source], dst_ref=att_recv.at[:, :, target],
            send_sem=sect_send.at[SHARED + cross], recv_sem=sect_recv.at[SHARED],
            device_id=to_cross if cross else to_sect, device_id_type=MESH,
        )

    lat_own = pltpu.make_async_copy(
        lat_hbm.at[:, pl.ds(pl.multiple_of((2 * s + q) * quarter, HEAD_DIM), quarter)],
        lat.at[0], lat_sem.at[0],
    )

    def lat_copy(cross):
        section = 1 - s if cross else s
        source = pl.ds(pl.multiple_of((2 * section + 1 - q) * quarter, HEAD_DIM), quarter)
        return pltpu.make_async_remote_copy(
            src_ref=lat_hbm.at[:, source], dst_ref=lat.at[1],
            send_sem=lat_send.at[cross], recv_sem=lat_recv.at[0],
            device_id=to_cross if cross else to_seq, device_id_type=MESH,
        )

    gate_copy = pltpu.make_async_remote_copy(
        src_ref=gate_ref, dst_ref=gate_recv, send_sem=gate_send.at[0],
        recv_sem=gate_recv_sem.at[0], device_id=to_sect, device_id_type=MESH,
    )
    pieces = ((0, 2 * part), (2 * part, rest))

    def tail_copy(jj):
        piece = pl.ds(*pieces[jj])
        return pltpu.make_async_remote_copy(
            src_ref=tail.at[:, piece], dst_ref=prev.at[:, piece],
            send_sem=tail_send.at[jj], recv_sem=tail_recv.at[jj],
            device_id=to_next, device_id_type=MESH,
        )

    barrier = pltpu.get_barrier_semaphore()
    pl.semaphore_signal(barrier, inc=1, device_id=to_seq, device_id_type=MESH)
    pl.semaphore_signal(barrier, inc=1, device_id=to_sect, device_id_type=MESH)

    @pl.when(inner)
    def _():
        pl.semaphore_signal(barrier, inc=1, device_id=to_cross, device_id_type=MESH)

    @pl.when(has_next)
    def _():
        pl.semaphore_signal(barrier, inc=1, device_id=to_next, device_id_type=MESH)

    @pl.when(has_prev)
    def _():
        pl.semaphore_signal(
            barrier, inc=1, device_id={"span": jnp.maximum(c - 1, 0)}, device_id_type=MESH
        )

    neighbours = 2 + sum(jnp.where(x, 1, 0) for x in (inner, has_next, has_prev))
    pl.semaphore_wait(barrier, neighbours)

    def takes_part(n, cond):
        return cond & inner if n == SHARED else cond

    def straight_near(n):
        @pl.when(takes_part(n, has_next & (q == 1)))
        def _():
            for i in range(2):
                near_copy(n, i, True).start()

    def start_seq(n, i):
        if n == SHARED:
            @pl.when(outer)
            def _():
                seq_copy(n, i).start()

            if i == 0:
                @pl.when(inner)
                def _():
                    lat_copy(0).start()
        elif n < SLOTS:
            seq_copy(n, i).start()

    def start_own(n):
        for i in range(3):
            own_copy(n, i).start()

    for i in range(3):
        start_seq(0, i)
    straight_near(0)
    gate_copy.start()
    for n in range(SLOTS):
        if n == SHARED:
            @pl.when(inner)
            def _():
                start_own(SHARED)
                lat_copy(1).start()
        else:
            start_own(n)
    lat_own.start()

    earlier = jnp.maximum(c - 1, 0)
    reach = jnp.where(has_prev, window_ref[earlier], 0)
    first_open = rows - reach * TOK_FRAME
    open_rows = lax.broadcasted_iota(jnp.int32, (rows, HEAD_DIM), 0) >= first_open
    ones = jnp.ones((rows, HEAD_DIM), jnp.bfloat16)
    v_ext[0, :, HEAD_DIM:] = ones
    v_ext[1, :, HEAD_DIM:] = ones
    v_ext[2, :, HEAD_DIM:] = jnp.where(open_rows, 1.0, 0.0).astype(jnp.bfloat16)

    @pl.when(jnp.logical_not(has_prev))
    def _():
        near_k[...] = jnp.zeros_like(near_k)
        near_v[...] = jnp.zeros_like(near_v)
        prev[...] = jnp.zeros_like(prev)

    factor = math.log2(math.e) / math.sqrt(HEAD_DIM)

    def attend(n):
        def one_head(head, carry):
            at = pl.multiple_of(head * HEAD_DIM, HEAD_DIM)
            lanes = pl.ds(at, HEAD_DIM)
            open_now = lax.broadcasted_iota(jnp.int32, (rows, HEAD_DIM), 0) >= first_open
            spare = k_buf[n, 0, :, lanes][:8].astype(jnp.float32)[:1]
            k_mask[...] = jnp.where(
                open_now, near_k[n, :, lanes].astype(jnp.float32), spare
            ).astype(jnp.bfloat16)
            v_ext[0, :, :HEAD_DIM] = v_buf[n, 0, :, lanes]
            v_ext[1, :, :HEAD_DIM] = v_buf[n, 1, :, lanes]
            v_ext[2, :, :HEAD_DIM] = jnp.where(
                open_now, near_v[n, :, lanes].astype(jnp.float32), 0.0
            ).astype(jnp.bfloat16)

            def one_side(who, carry):
                query = q_buf[n, who, :, lanes]
                keys = (k_buf[n, 0, :, lanes], k_buf[n, 1, :, lanes], k_mask[...])
                scores = [
                    lax.dot_general(
                        query, key, (((1,), (1,)), ((), ())), preferred_element_type=jnp.float32
                    )
                    for key in keys
                ]
                top = functools.reduce(
                    jnp.maximum, [jnp.max(x, axis=-1, keepdims=True) for x in scores]
                )
                total = None
                for m, x in enumerate(scores):
                    lifted = jnp.exp2((x - top) * factor).astype(jnp.bfloat16)
                    term = jnp.dot(lifted, v_ext[m], preferred_element_type=jnp.float32)
                    total = term if total is None else total + term
                result = (total[:, :HEAD_DIM] / total[:, HEAD_DIM:]).astype(jnp.bfloat16)
                side = lax.rem(who + q, 2)
                if n <= SHARED:
                    att_far[n, side, :, lanes] = result
                else:
                    here = pl.multiple_of((n - 3) * part + at, HEAD_DIM)
                    att_own[side, :, pl.ds(here, HEAD_DIM)] = result
                return carry

            return lax.fori_loop(0, 2, one_side, carry)

        lax.fori_loop(0, breadth(n) // HEAD_DIM, one_head, 0)

    def finish(jj):
        def block(step, carry):
            at = pl.multiple_of(pieces[jj][0] + step * HEAD_DIM, HEAD_DIM)
            lanes = pl.ds(at, HEAD_DIM)
            spot = pl.ds(pl.multiple_of((2 * s + q) * quarter + at, HEAD_DIM), HEAD_DIM)
            gate_own, gate_other = gate_ref[:, spot], gate_recv[:, spot]
            for side in range(2):
                gated_own = gate_own * att_own[side, :, lanes].astype(jnp.float32)
                gated_other = gate_other * att_recv[side, :, lanes].astype(jnp.float32)
                first = jnp.where(s == 0, gated_own, gated_other)
                later = jnp.where(s == 0, gated_other, gated_own)
                base = lat[lax.rem(side + q, 2), :, lanes].astype(jnp.float32)
                after_one = (base + first).astype(jnp.bfloat16)
                result = after_one.astype(jnp.float32) + later
                second[side, :, lanes] = result.astype(jnp.bfloat16)
                if side == 1:
                    tail[:, lanes] = result[rows - tail_rows:].astype(jnp.bfloat16)
            return carry

        lax.fori_loop(0, pieces[jj][1] // HEAD_DIM, block, 0)

        @pl.when(has_next)
        def _():
            tail_copy(jj).start()

    def ready(n):
        for i in range(3):
            own_copy(n, i).wait()

        @pl.when(has_prev)
        def _():
            for i in range(2):
                near_copy(n, i, False).wait_recv()

        attend(n)

    for n in range(SLOTS):
        for i in range(3):
            if n == SHARED:
                @pl.when(inner)
                def _():
                    seq_copy(n, i).wait_recv()

                @pl.when(outer)
                def _():
                    seq_copy(n, i).wait_send()
            else:
                seq_copy(n, i).wait_recv()
            start_seq(n + 1, i)
            if i < 2:
                @pl.when(takes_part(n, has_next & (q == 0)))
                def _():
                    near_copy(n, i, False).start()
        if n < LAST:
            straight_near(n + 1)
        if n == SHARED:
            @pl.when(inner)
            def _():
                ready(SHARED)
                for cross in range(2):
                    shared_copy(cross).start()
        else:
            ready(n)
        if n < SHARED:
            sect_copy(n).start()
        if n == LAST - 1:
            gate_copy.wait_recv()
            lat_own.wait()
            lat_copy(0).wait_recv()
            for m in range(SHARED):
                sect_copy(m).wait_recv()
            shared_copy(0).wait_recv()
            finish(0)
    finish(1)
    for jj in range(2):
        @pl.when(has_prev)
        def _():
            tail_copy(jj).wait_recv()

    @pl.when(inner)
    def _():
        for cross in range(2):
            shared_copy(cross).wait_send()
            lat_copy(cross).wait_send()

    for n in range(SHARED):
        sect_copy(n).wait_send()
    gate_copy.wait_send()
    for n in range(SLOTS):
        if n != SHARED:
            for i in range(3):
                seq_copy(n, i).wait_send()

        @pl.when(takes_part(n, has_next))
        def _():
            for i in range(2):
                near_copy(n, i, False).wait_send()

    @pl.when(has_next)
    def _():
        for jj in range(2):
            tail_copy(jj).wait_send()


def blend_kernel(second, prev, inter_ref, blend_ref, out):
    c = lax.axis_index("span")
    earlier = jnp.maximum(c - 1, 0)
    length = jnp.where(c > 0, inter_ref[earlier], 0)
    out[...] = second[...]

    def frame(f, carry):
        source = pl.ds(pl.multiple_of((BF - length + f) * TOK_FRAME, 16), TOK_FRAME)
        here = pl.ds(pl.multiple_of(f * TOK_FRAME, 16), TOK_FRAME)
        weight = (blend_ref[earlier, f].astype(jnp.float32) + 0.5) / WEIGHTS
        leading = second[0, here, :].astype(jnp.float32)
        mixed = weight * leading + (1.0 - weight) * prev[source, :].astype(jnp.float32)
        out[0, here, :] = mixed.astype(jnp.bfloat16)
        return carry

    lax.fori_loop(0, length, frame, 0)


def local(
    latents, queries, key_states, value_states, gate_scales, window, intersection, blend_index
):
    rows, width = latents.shape
    quarter = width // 4
    part = quarter // HEAD_DIM * 2 // 5 * HEAD_DIM
    spans = lax.axis_size("span")
    tail_rows = BF * TOK_FRAME
    wide = jnp.bfloat16
    dma = pltpu.SemaphoreType.DMA
    flops = 4 * 2 * rows * 3 * rows * width // 2
    smem = pl.BlockSpec(memory_space=pltpu.SMEM)
    vmem = pl.BlockSpec(memory_space=pltpu.VMEM)
    second, prev = pl.pallas_call(
        functools.partial(kernel, spans),
        out_shape=(
            jax.ShapeDtypeStruct((2, rows, quarter), wide),
            jax.ShapeDtypeStruct((tail_rows, quarter), wide),
        ),
        in_specs=[pl.BlockSpec(memory_space=pl.ANY)] * 4 + [vmem, smem],
        out_specs=(vmem, vmem),
        scratch_shapes=[
            pltpu.VMEM((SLOTS, 2, rows, part), wide),
            pltpu.VMEM((SLOTS, 2, rows, part), wide),
            pltpu.VMEM((SLOTS, 2, rows, part), wide),
            pltpu.VMEM((SLOTS, rows, part), wide),
            pltpu.VMEM((SLOTS, rows, part), wide),
            pltpu.VMEM((SHARED + 1, 2, rows, part), wide),
            pltpu.VMEM((2, rows, quarter), wide),
            pltpu.VMEM((2, rows, quarter), wide),
            pltpu.VMEM((2, rows, quarter), wide),
            pltpu.VMEM((tail_rows, quarter), wide),
            pltpu.VMEM(gate_scales.shape, jnp.float32),
            pltpu.VMEM((3, rows, 2 * HEAD_DIM), wide),
            pltpu.VMEM((rows, HEAD_DIM), wide),
            dma((SLOTS, 3)), dma((1,)), dma((SLOTS, 3)), dma((SLOTS, 3)),
            dma((2,)), dma((1,)), dma((SLOTS, 2)), dma((SLOTS, 2)),
            dma((SHARED + 2,)), dma((SHARED + 1,)), dma((1,)), dma((1,)), dma((2,)), dma((2,)),
        ],
        cost_estimate=pl.CostEstimate(
            flops=flops, bytes_accessed=8 * rows * width, transcendentals=flops // 512
        ),
        compiler_params=pltpu.CompilerParams(
            collective_id=0, has_side_effects=True, vmem_limit_bytes=60 * 1024 * 1024
        ),
    )(latents, queries, key_states, value_states, gate_scales, window)
    block = 2 * HEAD_DIM
    result = pl.pallas_call(
        blend_kernel,
        grid=(quarter // block,),
        out_shape=jax.ShapeDtypeStruct((2, rows, quarter), wide),
        in_specs=[
            pl.BlockSpec((2, rows, block), lambda i: (0, 0, i)),
            pl.BlockSpec((tail_rows, block), lambda i: (0, i)),
            smem,
            smem,
        ],
        out_specs=pl.BlockSpec((2, rows, block), lambda i: (0, 0, i)),
        compiler_params=pltpu.CompilerParams(vmem_limit_bytes=16 * 1024 * 1024),
    )(second, prev, intersection, blend_index)
    return result.reshape(2 * rows, quarter)


def solution(mesh):
    in_specs = (
        P(("span", "seq"), None),
        P("section", ("span", "seq"), None),
        P("section", ("span", "seq"), None),
        P("section", ("span", "seq"), None),
        P("section", None),
        P(),
        P(),
        P(),
    )
    out_specs = P("span", ("section", "seq"))
    return jax.shard_map(local, mesh=mesh, in_specs=in_specs, out_specs=out_specs, check_vma=False)
```

time: 277 us -> 275 us (level)
  other arithmetic: 5.2 us -> 0 us
  Pallas kernels: 267 us -> 272 us
    pallas_call x0 -> x1, Pallas kernels: none -> 3.58 us  [local(): pl.pallas_call(blend_kernel, grid=(quarter // block,), out_shape=jax.Shap...]
    unnamed x2 -> x8, local copies, waits for them, and re-layouts: 0.01 us -> 3.02 us
where the time goes in v2:
time: 275 us
  Pallas kernels  272 us (99%)
  local copies, waits for them, and re-layouts  3.02 us (1%)
    pallas_call x1, Pallas kernels, local(): pl.pallas_call(functools.partial(kernel, spans), out_shape=(jax.ShapeDtyp...  268 us

profile of v2, /device:TPU:4, one launch (start us, length us, event | category | flops | bytes accessed | tf_op | source)
XLA Modules:
  0.0 274.9 jit_solution(1117479914032586342)
XLA Ops:
  0.0 0.0 copy-start.2
  0.0 0.0 copy-start.3
  0.0 268.3 %shard_map.82 = (bf16[2,504,1280]{2,1,0:T(8,128)(2,1)}, bf16[480,1280]{1,0:T(8,128)(2,1)}) custom-call(bf16[504,5120]{1,0:T(8,128)(2,1)} %lat_hbm.1, bf16[1,504,5120]{2,1,0:T(8,128)(2,1)} %q_hbm.1, bf16[1,504,5120]{2,1,0:T(8,128)(2,1)} %k_hbm.1, bf16[1,504,5120]{2,1,0:T(8,128)(2,1)} %v_hbm.1, f32[1,5120]{1,0:T(1,128)} %gate_ref.1, s32[7]{0:T(128)} %window_ref.1), custom_call_target="tpu_custom_call" | custom-call | flops 15606743040 | bytes 20643840 | tf_op jit(solution)/shard_map/pallas_call | solution.py:389
  268.3 0.0 copy-done.2
  268.3 0.0 copy-done.3
  268.3 0.0 copy-start
  268.3 1.7 copy-done
  270.1 0.0 copy-start.1
  270.1 1.3 copy-done.1
  271.4 3.6 %shard_map.83 = bf16[2,504,1280]{2,1,0:T(8,128)(2,1)} custom-call(bf16[2,504,1280]{2,1,0:T(8,128)(2,1)S(1)} %copy-done, bf16[480,1280]{1,0:T(8,128)(2,1)S(1)} %copy-done.1, s32[7]{0:T(128)S(1)} %copy-done.3, s32[7,10]{1,0:T(8,128)S(1)} %copy-done.2), custom_call_target="tpu_custom_call" | custom-call | tf_op jit(solution)/shard_map/pallas_call | solution.py:423
Async XLA Ops:
  0.0 268.3 %copy-start.2 = (s32[7,10]{1,0:T(8,128)S(1)}, s32[7,10]{1,0:T(8,128)}, u32[]{:S(2)}) copy-start(s32[7,10]{1,0:T(8,128)} %blend_ref.1) | copy-start | bytes 844
  0.0 268.3 %copy-start.3 = (s32[7]{0:T(128)S(1)}, s32[7]{0:T(128)}, u32[]{:S(2)}) copy-start(s32[7]{0:T(128)} %inter_ref.1) | copy-start | bytes 88
  268.3 1.7 copy-start
  270.1 1.3 copy-start.1

commit v3 on v2

--- a/solution.py
+++ b/solution.py
@@ -15,6 +15,7 @@
 SLOTS = 6
 SHARED = 2
 LAST = SLOTS - 1
+IN_FLIGHT = 5
 MESH = pl.DeviceIdType.MESH
 
 
@@ -168,16 +169,20 @@
                 @pl.when(inner)
                 def _():
                     lat_copy(0).start()
-        elif n < SLOTS:
+        else:
             seq_copy(n, i).start()
 
     def start_own(n):
         for i in range(3):
             own_copy(n, i).start()
 
-    for i in range(3):
-        start_seq(0, i)
+    order = [(0, 0), (0, 1)]
+    for n in range(SLOTS):
+        order += [(n + 1, 0), (n + 1, 1), (n, 2)] if n < LAST else [(n, 2)]
+    for item in order[:IN_FLIGHT]:
+        start_seq(*item)
     straight_near(0)
+    straight_near(1)
     gate_copy.start()
     for n in range(SLOTS):
         if n == SHARED:
@@ -287,25 +292,35 @@
 
         attend(n)
 
+    def arrive(n, i):
+        if n == SHARED:
+            @pl.when(inner)
+            def _():
+                seq_copy(n, i).wait_recv()
+
+            @pl.when(outer)
+            def _():
+                seq_copy(n, i).wait_send()
+        else:
+            seq_copy(n, i).wait_recv()
+        following = order.index((n, i)) + IN_FLIGHT
+        if following < len(order):
+            start_seq(*order[following])
+        if i < 2:
+            @pl.when(takes_part(n, has_next & (q == 0)))
+            def _():
+                near_copy(n, i, False).start()
+
     for n in range(SLOTS):
-        for i in range(3):
-            if n == SHARED:
-                @pl.when(inner)
-                def _():
-                    seq_copy(n, i).wait_recv()
-
-                @pl.when(outer)
-                def _():
-                    seq_copy(n, i).wait_send()
-            else:
-                seq_copy(n, i).wait_recv()
-            start_seq(n + 1, i)
-            if i < 2:
-                @pl.when(takes_part(n, has_next & (q == 0)))
-                def _():
-                    near_copy(n, i, False).start()
+        if n == 0:
+            arrive(0, 0)
+            arrive(0, 1)
         if n < LAST:
-            straight_near(n + 1)
+            arrive(n + 1, 0)
+            arrive(n + 1, 1)
+        if n < LAST - 1:
+            straight_near(n + 2)
+        arrive(n, 2)
         if n == SHARED:
             @pl.when(inner)
             def _():
@@ -431,7 +446,7 @@
             smem,
         ],
         out_specs=pl.BlockSpec((2, rows, block), lambda i: (0, 0, i)),
-        compiler_params=pltpu.CompilerParams(vmem_limit_bytes=16 * 1024 * 1024),
+        compiler_params=pltpu.CompilerParams(vmem_limit_bytes=60 * 1024 * 1024),
     )(second, prev, intersection, blend_index)
     return result.reshape(2 * rows, quarter)
 

time: 275 us -> 273 us (level)
  local copies, waits for them, and re-layouts: 3.02 us -> 0 us
    unnamed x8 -> x0, local copies, waits for them, and re-layouts: 3.02 us -> none
where the time goes in v3:
time: 273 us; the launch traced here: 272 us
  Pallas kernels  272 us (100%)
    pallas_call x1, Pallas kernels, local(): pl.pallas_call(functools.partial(kernel, spans), out_shape=(jax.ShapeDtyp...  267 us

profile of v3, /device:TPU:4, one launch (start us, length us, event | category | flops | bytes accessed | tf_op | source)
XLA Modules:
  0.0 272.5 jit_solution(7169974910384949822)
XLA Ops:
  0.0 267.3 %shard_map.82 = (bf16[2,504,1280]{2,1,0:T(8,128)(2,1)}, bf16[480,1280]{1,0:T(8,128)(2,1)}) custom-call(bf16[504,5120]{1,0:T(8,128)(2,1)} %lat_hbm.1, bf16[1,504,5120]{2,1,0:T(8,128)(2,1)} %q_hbm.1, bf16[1,504,5120]{2,1,0:T(8,128)(2,1)} %k_hbm.1, bf16[1,504,5120]{2,1,0:T(8,128)(2,1)} %v_hbm.1, f32[1,5120]{1,0:T(1,128)} %gate_ref.1, s32[7]{0:T(128)} %window_ref.1), custom_call_target="tpu_custom_call" | custom-call | flops 15606743040 | bytes 20643840 | tf_op jit(solution)/shard_map/pallas_call | solution.py:404
  267.3 5.2 %shard_map.83 = bf16[2,504,1280]{2,1,0:T(8,128)(2,1)} custom-call(bf16[2,504,1280]{2,1,0:T(8,128)(2,1)} %get-tuple-element.7.second, bf16[480,1280]{1,0:T(8,128)(2,1)} %get-tuple-element.8.prev, s32[7]{0:T(128)} %inter_ref.1, s32[7,10]{1,0:T(8,128)} %blend_ref.1), custom_call_target="tpu_custom_call" | custom-call | tf_op jit(solution)/shard_map/pallas_call | solution.py:438
